TPU v7x, 32 devices: a whole 2x2x4 slice. The times are simulated.
32 devices in a mesh: group: 2 (over y), tile: 4 (over z), head: 4 (over x, core).
Axes of the slice: x: 2, y: 2, z: 4, core: 2. Of those that a mesh axis runs over, the one named last changes fastest.
Arguments:
- latent: bfloat16 [32, 6, 32, 3072], P(('group', 'tile'), None, None, 'head'), parts along dimension 0, may hold values from -6 to 6
- text_tokens: bfloat16 [512, 3072], P('group'), parts along dimension 0, may hold values from -6 to 6
- mod_shift: float32 [3072], replicated, may hold values from -3 to 3
- mod_scale: float32 [3072], replicated, may hold values from -2.5 to 2.5
- mod_gate: float32 [3072], replicated, may hold values from 0.5 to 2
- project_in: bfloat16 [3072, 3, 3072], P(None, None, 'head')
- project_out: bfloat16 [3072, 3072], P('head'), may hold values from -0.109375 to 0.109375
- q_gain: float32 [128], replicated, may hold values from 0.7 to 7
- k_gain: float32 [128], replicated, may hold values from 0.7 to 7
- pattern: int32 [8, 4], P('tile'), may hold values from 0 to 5, as said below
- tile_rows: int32 [16], P('group'), parts along dimension 0, may hold values from 96 to 384, as said below
- text_mask: int32 [512], P('group'), parts along dimension 0, may hold values from 0 to 1, as said below
Outputs:
- update: bfloat16 [32, 6, 32, 3072], P(('group', 'head'), None, 'tile'), parts along dimension 0
- text_update: bfloat16 [512, 3072], P(('group', 'head')), parts along dimension 0
There are 2 independent parts, one for each index of `group`. A program takes and returns all parts, laid end to end along the dimension named above; an argument that names none is the same for every part. Nothing has to cross between parts.
Inputs may be any that keep to these rules, and one draw needn't show every extreme that they name: `pattern`: entries of a row are distinct, the first is the query tile itself (s = 2 + its index in its band), and none names a band outside the grid. `tile_rows`: tiles of the last column band hold from 96 to 384 real tokens; every other tile holds 384. `text_mask`: the ones form a prefix of at least 32 positions.
All inputs are finite; a program needn't handle non-finite values.
Results may differ from a plain program's by a relative error of at most 0.015.
The roundings to bfloat16 on the way count: a program that leaves them out, or rounds other values in their place, can miss the bound.
Values may be sent and summed in bfloat16 or wider, within the bound.
A program may use at most 128 MiB of HBM per device.

v0:
```python
import functools
import math

import jax
import jax.numpy as jnp
from jax import lax
from jax.experimental import pallas as pl
from jax.experimental.pallas import tpu as pltpu
from jax.sharding import PartitionSpec as P

D = 3072
HD = 128
F = 16
H = 6
TF = 8
TH = 6
TW = 8
TEXT = 256


EPSILON = 1e-06


def modulate(values, mod_shift, mod_scale):
    widened = values.astype(jnp.float32)
    center = jnp.mean(widened, axis=-1, keepdims=True)
    offset = widened - center
    variance = jnp.mean(offset * offset, axis=-1, keepdims=True)
    return (offset * lax.rsqrt(variance + EPSILON) * (1.0 + mod_scale) + mod_shift).astype(
        jnp.bfloat16
    )


def rms_gain(values, gains):
    square = jnp.mean(values * values, axis=-1, keepdims=True)
    return (values * lax.rsqrt(square + EPSILON) * gains).astype(jnp.bfloat16)


def prepare(normed, project_in, q_gain, k_gain):
    product = jnp.einsum("td,dcn->tcn", normed, project_in, preferred_element_type=jnp.float32)
    count, _, width = product.shape

    def heads_of(index):
        return product[:, index].reshape(count, width // HD, HD)

    query_part = rms_gain(heads_of(0), q_gain).reshape(count, width)
    key_part = rms_gain(heads_of(1), k_gain).reshape(count, width)
    return (query_part, key_part, product[:, 2].astype(jnp.bfloat16))


SCALE = math.log2(math.e) / math.sqrt(HD)
MASKED = -1e30


def softmax_blend(queries, chunks):
    logits = []
    for keys, _, bias in chunks:
        raw = lax.dot_general(
            queries, keys, (((1,), (1,)), ((), ())), preferred_element_type=jnp.float32
        )
        logits.append(raw * SCALE + bias)
    highest = jnp.max(logits[0], axis=-1, keepdims=True)
    for part in logits[1:]:
        highest = jnp.maximum(highest, jnp.max(part, axis=-1, keepdims=True))
    sums = None
    blended = None
    for part, (_, values, _) in zip(logits, chunks):
        weights = jnp.exp2(part - highest)
        row = jnp.sum(weights, axis=-1, keepdims=True)
        term = jnp.dot(
            weights.astype(jnp.bfloat16), values, preferred_element_type=jnp.float32
        )
        sums = row if sums is None else sums + row
        blended = term if blended is None else blended + term
    return highest, sums, blended


def latent_kernel(per_device, tile_size, slots, rows_ref, q_ref, own_k, own_v, low_k, low_v,
                  high_k, high_v, text_k, text_v, bias_ref, text_bias, out_ref, keys, values):
    for band, (k_ref, v_ref) in enumerate(((low_k, low_v), (own_k, own_v), (high_k, high_v))):
        for local in range(per_device):
            rows = pl.ds(local * tile_size, tile_size)
            keys[band * per_device + local] = k_ref[rows, :]
            values[band * per_device + local] = v_ref[rows, :]
    for local in range(per_device):
        rows = pl.ds(local * tile_size, tile_size)
        chunks = []
        for s in range(slots):
            slot = rows_ref[1 + local, s]
            chunks.append((keys[slot], values[slot], bias_ref[local, s]))
        chunks.append((text_k[...], text_v[...], text_bias[...]))
        _, sums, blended = softmax_blend(q_ref[rows, :], chunks)
        place = lax.broadcasted_iota(jnp.int32, (tile_size, HD), 0)
        out_ref[rows, :] = jnp.where(
            place < rows_ref[0, local], blended / sums, 0.0
        ).astype(jnp.bfloat16)


def text_kernel(q_ref, own_k, own_v, text_k, text_v, own_bias, text_bias, out_ref, level_ref):
    chunks = (
        (own_k[...], own_v[...], own_bias[...]),
        (text_k[...], text_v[...], text_bias[...]),
    )
    highest, sums, blended = softmax_blend(q_ref[...], chunks)
    out_ref[...] = (blended / sums).astype(jnp.bfloat16)
    level_ref[...] = jnp.broadcast_to(highest + jnp.log2(sums), level_ref.shape)


def column(rows):
    return pl.BlockSpec((rows, HD), lambda head, *_: (0, head))


def fixed(shape):
    return pl.BlockSpec(shape, lambda head, *_: (0,) * len(shape))


def shards(
    latent,
    text_tokens,
    mod_shift,
    mod_scale,
    mod_gate,
    project_in,
    project_out,
    q_gain,
    k_gain,
    pattern,
    tile_rows,
    text_mask,
):
    head_count = lax.axis_size("head")
    band_count = lax.axis_size("tile")
    band_index = lax.axis_index("tile")
    moved = lax.all_to_all(latent, "tile", split_axis=2, concat_axis=0, tiled=True)
    column_whole = lax.all_gather(moved, "head", axis=3, tiled=True)
    normed = modulate(column_whole, mod_shift, mod_scale).reshape(-1, D)
    own_q, own_k, own_v = prepare(normed, project_in, q_gain, k_gain)
    text_q, text_k, text_v = prepare(
        modulate(text_tokens, mod_shift, mod_scale), project_in, q_gain, k_gain
    )
    count, width = own_q.shape
    local_heads = width // HD
    per_device = F // TF * (H // TH)
    tile_size = TF * TH * TW
    slots = pattern.shape[1]
    forward = [(i, i + 1) for i in range(band_count - 1)]
    backward = [(target, source) for source, target in forward]
    low_k, low_v = (lax.ppermute(part, "tile", forward) for part in (own_k, own_v))
    high_k, high_v = (lax.ppermute(part, "tile", backward) for part in (own_k, own_v))

    positions = jnp.arange(tile_size, dtype=jnp.int32)
    text_usable = text_mask == 1
    slot_band = band_index + pattern // per_device - 1
    picked_rows = tile_rows[
        jnp.clip(slot_band, 0, band_count - 1) * per_device + pattern % per_device
    ]
    bias = jnp.where(positions < picked_rows[..., None], 0.0, MASKED).astype(jnp.float32)
    bias = bias.reshape(per_device, slots, 1, tile_size)
    text_bias = jnp.where(text_usable, 0.0, MASKED).astype(jnp.float32)[None]
    own_rows = lax.dynamic_slice_in_dim(tile_rows, band_index * per_device, per_device, 0)
    own_bias = jnp.where(positions[None] < own_rows[:, None], 0.0, MASKED)
    own_bias = own_bias.astype(jnp.float32).reshape(1, count)
    once_bias = jnp.where(band_index == 0, text_bias, MASKED)

    text_part, levels = pl.pallas_call(
        text_kernel,
        grid=(local_heads,),
        in_specs=[
            column(TEXT), column(count), column(count), column(TEXT), column(TEXT),
            fixed((1, count)), fixed((1, TEXT)),
        ],
        out_specs=[column(TEXT), column(TEXT)],
        out_shape=[
            jax.ShapeDtypeStruct((TEXT, width), jnp.bfloat16),
            jax.ShapeDtypeStruct((TEXT, width), jnp.float32),
        ],
        compiler_params=pltpu.CompilerParams(vmem_limit_bytes=48 << 20),
        cost_estimate=pl.CostEstimate(
            flops=4 * TEXT * (count + TEXT) * width, bytes_accessed=6 << 20, transcendentals=0
        ),
        name="text_attention",
    )(text_q, own_k, own_v, text_k, text_v, own_bias, once_bias)
    level = levels.reshape(TEXT, local_heads, HD)[:, :, 0]
    distance = 1
    while distance < band_count:
        pairs = [(i, i ^ distance) for i in range(band_count)]
        other_part = lax.ppermute(text_part, "tile", pairs)
        other_level = lax.ppermute(level, "tile", pairs)
        peak = jnp.maximum(level, other_level)
        mine, theirs = jnp.exp2(level - peak), jnp.exp2(other_level - peak)
        total = mine + theirs

        def widen(share):
            return jnp.repeat(share, HD, axis=1)

        text_part = (
            text_part.astype(jnp.float32) * widen(mine / total)
            + other_part.astype(jnp.float32) * widen(theirs / total)
        ).astype(jnp.bfloat16)
        level = peak + jnp.log2(total)
        distance *= 2

    filler = jnp.zeros((1, slots - per_device), jnp.int32)
    numbers = jnp.concatenate(
        [jnp.concatenate([own_rows[None].astype(jnp.int32), filler], 1), pattern], 0
    )
    latent_out = pl.pallas_call(
        functools.partial(latent_kernel, per_device, tile_size, slots),
        grid_spec=pltpu.PrefetchScalarGridSpec(
            num_scalar_prefetch=1,
            grid=(local_heads,),
            in_specs=[column(count)] * 7 + [column(TEXT)] * 2
            + [fixed((per_device, slots, 1, tile_size)), fixed((1, TEXT))],
            out_specs=column(count),
            scratch_shapes=[pltpu.VMEM((3 * per_device, tile_size, HD), jnp.bfloat16)] * 2,
        ),
        out_shape=jax.ShapeDtypeStruct((count, width), jnp.bfloat16),
        compiler_params=pltpu.CompilerParams(vmem_limit_bytes=48 << 20),
        cost_estimate=pl.CostEstimate(
            flops=4 * count * (slots * tile_size + TEXT) * width,
            bytes_accessed=10 << 20, transcendentals=0,
        ),
        name="latent_attention",
    )(numbers, own_q, own_k, own_v, low_k, low_v, high_k, high_v, text_k, text_v, bias, text_bias)

    latent_columns = latent_out.reshape(head_count, -1, width)
    text_blocks = text_part.reshape(head_count, -1, width)
    latent_share = latent_columns.shape[1]
    joined = jnp.concatenate([latent_columns, text_blocks], 1).reshape(-1, width)
    summed_rows = lax.psum_scatter(
        jnp.dot(joined, project_out, preferred_element_type=jnp.float32).astype(jnp.bfloat16),
        "head",
        scatter_dimension=0,
        tiled=True,
    ).astype(jnp.float32)
    update = (
        (summed_rows[:latent_share] * mod_gate)
        .astype(jnp.bfloat16)
        .reshape(F // head_count, H, TW, D)
    )
    text_update = (summed_rows[latent_share:] * mod_gate).astype(jnp.bfloat16)
    return (update, text_update)


def solution(mesh):
    placed = (
        P(("group", "tile"), None, None, "head"),
        P("group", None),
        P(),
        P(),
        P(),
        P(None, None, "head"),
        P("head", None),
        P(),
        P(),
        P("tile", None),
        P("group"),
        P("group"),
    )
    return jax.shard_map(
        shards,
        mesh=mesh,
        in_specs=placed,
        out_specs=(P(("group", "head"), None, "tile", None), P(("group", "head"), None)),
        check_vma=False,
    )
```

profile of v0, /device:TPU:0, one launch (start us, length us, event | category | flops | bytes accessed | tf_op | source)
XLA Modules:
  0.0 326.7 jit_solution(15778242011204062684)
XLA Ops:
  7.2 1.9 copy.53
  9.1 43.1 %all_to_all.18 = bf16[4,6,32,768]{3,1,0,2:T(8,128)(2,1)S(1)} all-to-all(bf16[4,6,32,768]{3,1,0,2:T(8,128)(2,1)S(1)} %copy.53), channel_id=1, replica_groups=mesh['group'=2,'tile'=4,'head'=4] {'tile'}, dimensions={2} | all-to-all | bytes 2359296 | tf_op jit(solution)/shard_map/all_to_all | solution.py:134
  54.9 7.8 %fusion.18 = f32[256,3,768]{2,0,1:T(8,128)S(1)} fusion(bf16[3072,3,768]{2,0,1:T(8,128)(2,1)} %param.17, bf16[256,3072]{1,0:T(8,128)(2,1)S(1)} %copy-done.7, f32[3072]{0:T(1024)S(1)} %copy-done.16, f32[3072]{0:T(1024)S(1)} %broadcast_add_fusion, f32[256]{0:T(256)S(1)} %add_rsqrt_fusion.5, f32[256]{0:T(256)S(1)} %broadcast_multiply_fusion.1), kind=kOutput, calls=%fused_computation.30 | convolution fusion | flops 3628597248 | bytes 18114560 | tf_op jit(solution)/shard_map/td,dcn->tcn/dot_general | solution.py:40
  71.4 19.3 %all-gather.2.cloned.1.call-done = bf16[16,6,8,3072]{3,2,1,0:T(8,128)(2,1)} async-done(((bf16[16,6,8,768]{3,2,1,0:T(8,128)(2,1)}), bf16[16,6,8,3072]{3,2,1,0:T(8,128)(2,1)}) %all-gather.2.cloned.1.call-update) | async-done | bytes 4718608 | tf_op jit(solution)/shard_map/all_gather | solution.py:135
  90.7 3.2 convert_reduce_fusion
  95.8 2.7 fusion.5
  99.5 11.3 %fusion.37 = f32[768,3,768]{2,0,1:T(8,128)S(1)} fusion(bf16[768,3072,1]{1,0,2:T(8,128)(2,1)S(1)} %bitcast.90, bf16[3072,3,768]{2,0,1:T(8,128)(2,1)S(1)} %copy-done.23), kind=kOutput, calls=%fused_computation.90 | convolution fusion | flops 10871635968 | bytes 25952256 | tf_op jit(solution)/shard_map/td,dcn->tcn/dot_general | solution.py:40
  110.8 2.7 slice_multiply_fusion.2
  115.3 3.1 copy.58
  118.4 1.8 reduce_sum.74
  121.9 3.1 copy.59
  125.0 3.1 copy.61
  128.1 1.8 reduce_sum.75
  131.5 3.0 copy.62
  134.6 5.3 %fusion.16 = (bf16[768,768]{1,0:T(8,128)(2,1)}, bf16[768,768]{1,0:T(8,128)(2,1)S(1)}) fusion(f32[768,768]{1,0:T(8,128)} %copy.59, f32[768,3,768]{2,0,1:T(8,128)} %copy-done.6, f32[768]{0:T(1024)} %copy-done.13, f32[768]{0:T(1024)S(1)} %get-tuple-element.21, f32[768,768]{1,0:T(8,128)} %copy.62), kind=kLoop, calls=%fused_computation.26 | loop fusion | flops 3538944 | bytes 11802624 | tf_op jit(solution)/shard_map/convert_element_type | solution.py:36
  139.9 4.9 %text_attention.1 = (bf16[256,768]{1,0:T(8,128)(2,1)S(1)}, f32[256,768]{1,0:T(8,128)S(1)}) custom-call(bf16[256,768]{1,0:T(8,128)(2,1)S(1)} %get-tuple-element.11.q_ref, bf16[768,768]{1,0:T(8,128)(2,1)S(1)} %get-tuple-element.7.own_k, bf16[768,768]{1,0:T(8,128)(2,1)S(1)} %fusion.24.own_v, bf16[256,768]{1,0:T(8,128)(2,1)S(1)} %get-tuple-element.10.text_k, ...), custom_call_target="tpu_custom_call" | custom-call | flops 805306368 | bytes 6291456 | tf_op jit(solution)/shard_map/text_attention/pallas_call | solution.py:165
  146.4 2.3 copy.68
  151.6 4.4 %collective-permute-start = (bf16[768,768]{1,0:T(8,128)(2,1)S(1)}, bf16[768,768]{1,0:T(8,128)(2,1)}, u32[]{:S(2)}, u32[]{:S(2)}) collective-permute-start(bf16[768,768]{1,0:T(8,128)(2,1)S(1)} %get-tuple-element.7.own_k), channel_id=1, source_target_pairs={{0,4},{4,8},{8,12},{1,5},{5,9},{9,13},{2,6},{6,10},{10,14},{3,7},{... | collective-permute-start | bytes 3538952 | tf_op jit(solution)/shard_map/ppermute | solution.py:148
  157.4 5.6 %collective-permute-start.1 = (bf16[768,768]{1,0:T(8,128)(2,1)S(1)}, bf16[768,768]{1,0:T(8,128)(2,1)}, u32[]{:S(2)}, u32[]{:S(2)}) collective-permute-start(bf16[768,768]{1,0:T(8,128)(2,1)S(1)} %fusion.24.own_v), channel_id=1, source_target_pairs={{0,4},{4,8},{8,12},{1,5},{5,9},{9,13},{2,6},{6,10},{10,14},{3,7},{... | collective-permute-start | bytes 3538952 | tf_op jit(solution)/shard_map/ppermute | solution.py:148
  165.8 2.3 copy.69
  169.8 2.3 copy.70
  172.1 2.1 collective-permute-start.6
  174.1 2.4 add_convert_fusion.1
  176.5 34.6 %collective-permute-done.6 = f32[256,6]{0,1:T(8,128)S(1)} collective-permute-done((f32[256,6]{0,1:T(8,128)}, f32[256,6]{0,1:T(8,128)S(1)}, u32[]{:S(2)}, u32[]{:S(2)}) %collective-permute-start.6) | collective-permute-done | bytes 6176 | tf_op jit(solution)/shard_map/ppermute | solution.py:188
  211.1 3.4 %collective-permute-start.7 = (bf16[256,768]{1,0:T(8,128)(2,1)}, bf16[256,768]{1,0:T(8,128)(2,1)}, u32[]{:S(2)}, u32[]{:S(2)}) collective-permute-start(bf16[256,768]{1,0:T(8,128)(2,1)} %add_convert_fusion.1), channel_id=1, source_target_pairs={{0,8},{4,12},{8,0},{12,4},{1,9},{5,13},{9,1},{13,5},{2,10},{6,14},... | collective-permute-start | bytes 1179656 | tf_op jit(solution)/shard_map/ppermute | solution.py:187
  216.9 2.3 copy.71
  220.1 2.3 copy.72
  222.4 9.1 %collective-permute-done.7 = bf16[256,768]{1,0:T(8,128)(2,1)} collective-permute-done((bf16[256,768]{1,0:T(8,128)(2,1)}, bf16[256,768]{1,0:T(8,128)(2,1)}, u32[]{:S(2)}, u32[]{:S(2)}) %collective-permute-start.7) | collective-permute-done | bytes 393248 | tf_op jit(solution)/shard_map/ppermute | solution.py:187
  233.3 17.3 %latent_attention.1 = bf16[768,768]{1,0:T(8,128)(2,1)S(1)} custom-call(s32[3,4]{1,0:T(4,128)S(1)} %pad_add_fusion.rows_ref, bf16[768,768]{1,0:T(8,128)(2,1)S(1)} %copy-done, bf16[768,768]{1,0:T(8,128)(2,1)S(1)} %get-tuple-element.7.own_k, bf16[768,768]{1,0:T(8,128)(2,1)S(1)} %fusion.24.own_v, bf16[768,768]{1,0:T(8,128)(2,1)} %collective-permute-done.low_k, ...), custom_call_target="tpu_custom_call" | custom-call | flops 4227858432 | bytes 10485760 | tf_op jit(solution)/shard_map/latent_attention/pallas_call | solution.py:207
  250.7 7.1 %convolution_convert_fusion = bf16[1024,3072]{1,0:T(8,128)(2,1)} fusion(bf16[1024,768]{1,0:T(8,128)(2,1)S(1)} %bitcast.100, bf16[768,3072]{1,0:T(8,128)(2,1)S(1)} %bitcast.106), kind=kOutput, calls=%fused_computation.9 | convolution fusion | flops 4834983936 | bytes 12582912 | tf_op jit(solution)/shard_map/dot_general | solution.py:231
  257.9 58.2 %reduce-scatter.2.cloned.1.call-done = bf16[256,3072]{1,0:T(8,128)(2,1)} async-done(((bf16[1024,3072]{1,0:T(8,128)(2,1)}), bf16[256,3072]{1,0:T(8,128)(2,1)}) %reduce-scatter.2.cloned.1.call-update) | async-done | bytes 1572880 | tf_op jit(solution)/shard_map/reduce_scatter | solution.py:230
  316.1 1.8 convert_element_type.81
  (119 shorter events, 36.7 us)
Async XLA Ops:
  7.2 83.5 %all-gather.2.cloned.1.call-start = ((), (), s32[]{:S(2)}) async-start(), calls=%async_computation.2 | async-start | bytes 5898240 | tf_op jit(solution)/shard_map/all_gather | solution.py:135
  52.2 1.8 copy-start.7
  53.9 1.0 copy-start.16
  53.9 262.2 %reduce-scatter.2.cloned.1.call-start = ((), (), s32[]{:S(2)}) async-start(), calls=%async_computation.3 | async-start | bytes 7864320 | tf_op jit(solution)/shard_map/reduce_scatter | solution.py:230
  54.9 7.8 %copy-start.11 = (f32[3072]{0:T(1024)}, f32[3072]{0:T(1024)S(1)}, u32[]{:S(2)}) copy-start(f32[3072]{0:T(1024)S(1)} %broadcast_add_fusion) | copy-start | bytes 36868
  62.7 1.4 copy-start.8
  65.8 1.7 copy-start.18
  65.9 1.8 copy-start.4
  66.1 3.0 copy-start.19
  66.1 3.0 copy-start.21
  66.1 3.0 copy-start.22
  66.2 3.0 copy-start.9
  90.7 3.8 %copy-start.5 = (bf16[16,6,8,3072]{3,2,1,0:T(8,128)(2,1)S(1)}, bf16[16,6,8,3072]{3,2,1,0:T(8,128)(2,1)}, u32[]{:S(2)}) copy-start(bf16[16,6,8,3072]{3,2,1,0:T(8,128)(2,1)} %all-gather.2.cloned.1.call-done) | copy-start | bytes 14155780
  94.4 1.4 copy-start.12
  94.4 1.4 copy-start.17
  94.4 5.1 %copy-start.23 = (bf16[3072,3,768]{2,0,1:T(8,128)(2,1)S(1)}, bf16[3072,3,768]{2,0,1:T(8,128)(2,1)}, u32[]{:S(2)}) copy-start(bf16[3072,3,768]{2,0,1:T(8,128)(2,1)} %param.17) | copy-start | bytes 42467332
  110.8 4.4 %copy-start.6 = (f32[768,3,768]{2,0,1:T(8,128)}, f32[768,3,768]{2,0,1:T(8,128)S(1)}, u32[]{:S(2)}) copy-start(f32[768,3,768]{2,0,1:T(8,128)S(1)} %fusion.37) | copy-start | bytes 21233668
  139.9 11.7 %copy-start.20 = (s32[2,4]{1,0:T(2,128)S(1)}, s32[2,4]{1,0:T(2,128)}, u32[]{:S(2)}) copy-start(s32[2,4]{1,0:T(2,128)} %reshape.172) | copy-start | bytes 100
  149.5 13.4 %collective-permute-start.4 = (f32[256,6]{0,1:T(8,128)S(1)}, f32[256,6]{0,1:T(8,128)S(1)}, u32[]{:S(2)}, u32[]{:S(2)}) collective-permute-start(f32[256,6]{0,1:T(8,128)S(1)} %bitcast.104), channel_id=1, source_target_pairs={{0,4},{4,0},{8,12},{12,8},{1,5},{5,1},{9,13},{13,9},{2,6},{6,2},{1... | collective-permute-start | bytes 18440 | tf_op jit(solution)/shard_map/ppermute | solution.py:188
  151.0 21.0 %collective-permute-start.5 = (bf16[256,768]{1,0:T(8,128)(2,1)}, bf16[256,768]{1,0:T(8,128)(2,1)}, u32[]{:S(2)}, u32[]{:S(2)}) collective-permute-start(bf16[256,768]{1,0:T(8,128)(2,1)} %copy-done.2), channel_id=1, source_target_pairs={{0,4},{4,0},{8,12},{12,8},{1,5},{5,1},{9,13},{13,9},{2,6},{6,2},{1... | collective-permute-start | bytes 1179656 | tf_op jit(solution)/shard_map/ppermute | solution.py:187
  151.6 81.6 %collective-permute-start = (bf16[768,768]{1,0:T(8,128)(2,1)S(1)}, bf16[768,768]{1,0:T(8,128)(2,1)}, u32[]{:S(2)}, u32[]{:S(2)}) collective-permute-start(bf16[768,768]{1,0:T(8,128)(2,1)S(1)} %get-tuple-element.7.own_k), channel_id=1, source_target_pairs={{0,4},{4,8},{8,12},{1,5},{5,9},{9,13},{2,6},{6,10},{10,14},{3,7},{... | collective-permute-start | bytes 3538952 | tf_op jit(solution)/shard_map/ppermute | solution.py:148
  156.1 77.2 %collective-permute-start.2 = (bf16[768,768]{1,0:T(8,128)(2,1)S(1)}, bf16[768,768]{1,0:T(8,128)(2,1)}, u32[]{:S(2)}, u32[]{:S(2)}) collective-permute-start(bf16[768,768]{1,0:T(8,128)(2,1)S(1)} %get-tuple-element.7.own_k), channel_id=1, source_target_pairs={{4,0},{8,4},{12,8},{5,1},{9,5},{13,9},{6,2},{10,6},{14,10},{7,3},{... | collective-permute-start | bytes 3538952 | tf_op jit(solution)/shard_map/ppermute | solution.py:149
  157.4 75.9 %collective-permute-start.1 = (bf16[768,768]{1,0:T(8,128)(2,1)S(1)}, bf16[768,768]{1,0:T(8,128)(2,1)}, u32[]{:S(2)}, u32[]{:S(2)}) collective-permute-start(bf16[768,768]{1,0:T(8,128)(2,1)S(1)} %fusion.24.own_v), channel_id=1, source_target_pairs={{0,4},{4,8},{8,12},{1,5},{5,9},{9,13},{2,6},{6,10},{10,14},{3,7},{... | collective-permute-start | bytes 3538952 | tf_op jit(solution)/shard_map/ppermute | solution.py:148
  162.9 70.3 %collective-permute-start.3 = (bf16[768,768]{1,0:T(8,128)(2,1)S(1)}, bf16[768,768]{1,0:T(8,128)(2,1)}, u32[]{:S(2)}, u32[]{:S(2)}) collective-permute-start(bf16[768,768]{1,0:T(8,128)(2,1)S(1)} %fusion.24.own_v), channel_id=1, source_target_pairs={{4,0},{8,4},{12,8},{5,1},{9,5},{13,9},{6,2},{10,6},{14,10},{7,3},{... | collective-permute-start | bytes 3538952 | tf_op jit(solution)/shard_map/ppermute | solution.py:149
  164.9 9.3 %copy-start.3 = (bf16[256,768]{1,0:T(8,128)(2,1)S(1)}, bf16[256,768]{1,0:T(8,128)(2,1)}, u32[]{:S(2)}) copy-start(bf16[256,768]{1,0:T(8,128)(2,1)} %copy-done.2) | copy-start | bytes 1179652
  172.1 43.8 %copy-start.14 = (f32[256,6]{0,1:T(8,128)S(1)}, f32[256,6]{0,1:T(8,128)}, u32[]{:S(2)}) copy-start(f32[256,6]{0,1:T(8,128)} %get-tuple-element.17) | copy-start | bytes 18436
  172.1 39.0 %collective-permute-start.6 = (f32[256,6]{0,1:T(8,128)}, f32[256,6]{0,1:T(8,128)S(1)}, u32[]{:S(2)}, u32[]{:S(2)}) collective-permute-start(f32[256,6]{0,1:T(8,128)} %get-tuple-element.17), channel_id=1, source_target_pairs={{0,8},{4,12},{8,0},{12,4},{1,9},{5,13},{9,1},{13,5},{2,10},{6,14},... | collective-permute-start | bytes 18440 | tf_op jit(solution)/shard_map/ppermute | solution.py:188
  211.1 20.4 %collective-permute-start.7 = (bf16[256,768]{1,0:T(8,128)(2,1)}, bf16[256,768]{1,0:T(8,128)(2,1)}, u32[]{:S(2)}, u32[]{:S(2)}) collective-permute-start(bf16[256,768]{1,0:T(8,128)(2,1)} %add_convert_fusion.1), channel_id=1, source_target_pairs={{0,8},{4,12},{8,0},{12,4},{1,9},{5,13},{9,1},{13,5},{2,10},{6,14},... | collective-permute-start | bytes 1179656 | tf_op jit(solution)/shard_map/ppermute | solution.py:187
  222.4 10.9 %copy-start = (bf16[768,768]{1,0:T(8,128)(2,1)S(1)}, bf16[768,768]{1,0:T(8,128)(2,1)}, u32[]{:S(2)}) copy-start(bf16[768,768]{1,0:T(8,128)(2,1)} %get-tuple-element.6.q_ref) | copy-start | bytes 3538948
  233.3 17.4 %slice-start = ((s8[4718592]{0:T(1024)(128)(4,1)}), s8[4194304]{0:T(1024)(128)(4,1)S(1)}, s32[]{:S(2)}) async-start(s8[4718592]{0:T(1024)(128)(4,1)} %bitcast.105), calls=%async_computation.4 | async-start | bytes 8388608
  233.3 17.4 %slice-start.1 = ((s8[4718592]{0:T(1024)(128)(4,1)}), s8[524288]{0:T(1024)(128)(4,1)S(1)}, s32[]{:S(2)}) async-start(s8[4718592]{0:T(1024)(128)(4,1)} %bitcast.105), calls=%async_computation.5 | async-start | bytes 1048576
  257.8 60.0 %copy-start.10 = (f32[3072]{0:T(1024)S(1)}, f32[3072]{0:T(1024)}, u32[]{:S(2)}) copy-start(f32[3072]{0:T(1024)} %param.16) | copy-start | bytes 36868
  (4 other events, 3.2 us)
Sparse Core Ops, SparseCore 0:
  54.0 36.5 all-gather.1
  258.0 58.0 reduce-scatter.1
where the time goes:
time: 328 us; the launch traced here: 327 us
  waiting for transfers between devices  121 us (37%)
  local copies, waits for them, and re-layouts  48.3 us (15%)
  blocking collectives  43.1 us (13%)
  other arithmetic  31.1 us (9%)
  matrix products  26.2 us (8%)
  Pallas kernels  22.1 us (7%)
  starting transfers between devices  20.1 us (6%)
  between operations  14.5 us (4%)
    reduce_scatter x1, waiting for transfers between devices, shards(): lax.psum_scatter(jnp.dot(joined, project_out, preferred_element_type=jnp....  58.2 us
    all_to_all x1, blocking collectives, shards(): lax.all_to_all(latent, 'tile', split_axis=2, concat_axis=0, tiled=True)  43.1 us
    ppermute x2, waiting for transfers between devices, shards(): other_level = lax.ppermute(level, 'tile', pairs)  34.6 us
    all_gather x1, waiting for transfers between devices, shards(): column_whole = lax.all_gather(moved, 'head', axis=3, tiled=True)  19.3 us
    dot_general x2, matrix products, prepare(): jnp.einsum('td,dcn->tcn', normed, project_in, preferred_element_type=jnp....  19.1 us
    pallas_call x1, Pallas kernels, shards(): pl.pallas_call(functools.partial(latent_kernel, per_device, tile_size, sl...  17.3 us
    mul x9, local copies, waits for them, and re-layouts, rms_gain(): return (values * lax.rsqrt(square + EPSILON) * gains).astype(jnp.bfloat16)  11.9 us
    ppermute x2, starting transfers between devices, shards(): lax.ppermute(part, 'tile', forward)  10 us
  transfers between devices with their start and end apart: 10, of which 4 were waited for; matrix products, arithmetic and copies ran while one was open for 11% of the time, Pallas kernels for 0%

commit v1 on v0

--- a/solution.py
+++ b/solution.py
@@ -36,16 +36,31 @@
     return (values * lax.rsqrt(square + EPSILON) * gains).astype(jnp.bfloat16)
 
 
+def norm_kernel(product_ref, q_gain, k_gain, q_ref, k_ref, v_ref):
+    q_ref[...] = rms_gain(product_ref[0], q_gain[...])
+    k_ref[...] = rms_gain(product_ref[1], k_gain[...])
+    v_ref[...] = product_ref[2].astype(jnp.bfloat16)
+
+
 def prepare(normed, project_in, q_gain, k_gain):
-    product = jnp.einsum("td,dcn->tcn", normed, project_in, preferred_element_type=jnp.float32)
-    count, _, width = product.shape
-
-    def heads_of(index):
-        return product[:, index].reshape(count, width // HD, HD)
-
-    query_part = rms_gain(heads_of(0), q_gain).reshape(count, width)
-    key_part = rms_gain(heads_of(1), k_gain).reshape(count, width)
-    return (query_part, key_part, product[:, 2].astype(jnp.bfloat16))
+    product = jnp.einsum("td,dcn->ctn", normed, project_in, preferred_element_type=jnp.float32)
+    _, count, width = product.shape
+    return pl.pallas_call(
+        norm_kernel,
+        grid=(width // HD,),
+        in_specs=[
+            pl.BlockSpec((3, count, HD), lambda head: (0, 0, head)),
+            fixed((1, HD)),
+            fixed((1, HD)),
+        ],
+        out_specs=[column(count)] * 3,
+        out_shape=[jax.ShapeDtypeStruct((count, width), jnp.bfloat16)] * 3,
+        compiler_params=pltpu.CompilerParams(vmem_limit_bytes=32 << 20),
+        cost_estimate=pl.CostEstimate(
+            flops=8 * count * width, bytes_accessed=18 * count * width, transcendentals=0
+        ),
+        name="head_norm",
+    )(product, q_gain[None], k_gain[None])
 
 
 SCALE = math.log2(math.e) / math.sqrt(HD)

time: 328 us -> 302 us (0.921)
  local copies, waits for them, and re-layouts: 48.3 us -> 25.3 us
  other arithmetic: 31.1 us -> 17 us
  waiting for transfers between devices: 121 us -> 129 us
  Pallas kernels: 22.1 us -> 25.8 us
  matrix products: 26.2 us -> 29.5 us
    mul x13 -> x0, local copies, waits for them, and re-layouts: 18.6 us -> none  [the longest x9 11.9 us: rms_gain(): return (values * lax.rsqrt(square + EPSILON) * gains).astype(jnp.bfloat16)]
    convert_element_type x2 -> x0, other arithmetic: 6.92 us -> none  [rms_gain(): return (values * lax.rsqrt(square + EPSILON) * gains).astype(jnp.bfloat16)]
    pallas_call x0 -> x2, Pallas kernels: none -> 4.35 us  [prepare(): pl.pallas_call(norm_kernel, grid=(width // HD,), in_specs=[pl.BlockSpec((...]
    reduce_sum x4 -> x0, other arithmetic: 3.75 us -> none  [rms_gain(): square = jnp.mean(values * values, axis=-1, keepdims=True)]
    ppermute x2, waiting for transfers between devices: 34.6 us -> 38 us  [shards(): other_level = lax.ppermute(level, 'tile', pairs)]
    ppermute x2, starting transfers between devices: 3.92 us -> 0.57 us  [shards(): other_part = lax.ppermute(text_part, 'tile', pairs)]
    unnamed x55 -> x45, local copies, waits for them, and re-layouts: 8.85 us -> 7.02 us
  transfers between devices with their start and end apart: 10 -> 10, of which waited for: 4 -> 4; matrix products, arithmetic and copies ran while one was open for 11% -> 10% of each run, Pallas kernels for 0% -> 1%
where the time goes in v1:
time: 302 us; the launch traced here: 301 us
  waiting for transfers between devices  129 us (43%)
  blocking collectives  43.1 us (14%)
  matrix products  29.5 us (10%)
  Pallas kernels  25.8 us (9%)
  local copies, waits for them, and re-layouts  25.3 us (8%)
  starting transfers between devices  17.3 us (6%)
  other arithmetic  17 us (6%)
  between operations  14.4 us (5%)
    reduce_scatter x1, waiting for transfers between devices, shards(): lax.psum_scatter(jnp.dot(joined, project_out, preferred_element_type=jnp....  56.9 us
    all_to_all x1, blocking collectives, shards(): lax.all_to_all(latent, 'tile', split_axis=2, concat_axis=0, tiled=True)  43.1 us
    ppermute x2, waiting for transfers between devices, shards(): other_level = lax.ppermute(level, 'tile', pairs)  38 us
    all_gather x1, waiting for transfers between devices, shards(): column_whole = lax.all_gather(moved, 'head', axis=3, tiled=True)  22.4 us
    dot_general x2, matrix products, prepare(): jnp.einsum('td,dcn->ctn', normed, project_in, preferred_element_type=jnp....  20.1 us
    pallas_call x1, Pallas kernels, shards(): pl.pallas_call(functools.partial(latent_kernel, per_device, tile_size, sl...  16.6 us
    ppermute x2, waiting for transfers between devices, shards(): other_part = lax.ppermute(text_part, 'tile', pairs)  11.8 us
    dot_general x1, matrix products, shards(): jnp.dot(joined, project_out, preferred_element_type=jnp.float32)  9.31 us
  transfers between devices with their start and end apart: 10, of which 4 were waited for; matrix products, arithmetic and copies ran while one was open for 10% of the time, Pallas kernels for 1%

profile of v1, /device:TPU:0, one launch (start us, length us, event | category | flops | bytes accessed | tf_op | source)
XLA Modules:
  0.0 301.5 jit_solution(9961687690470983762)
XLA Ops:
  7.2 1.9 copy.25
  9.2 43.1 %all_to_all.18 = bf16[4,6,32,768]{3,1,0,2:T(8,128)(2,1)S(1)} all-to-all(bf16[4,6,32,768]{3,1,0,2:T(8,128)(2,1)S(1)} %copy.25), channel_id=1, replica_groups=mesh['group'=2,'tile'=4,'head'=4] {'tile'}, dimensions={2} | all-to-all | bytes 2359296 | tf_op jit(solution)/shard_map/all_to_all | solution.py:149
  52.3 1.7 copy.27
  56.5 8.8 %convolution_bitcast_fusion.1.product_ref = f32[3,256,768]{2,1,0:T(8,128)S(1)} fusion(bf16[3072,3,768]{2,0,1:T(8,128)(2,1)} %param.17, bf16[256,3072]{1,0:T(8,128)(2,1)} %param.13, f32[3072]{0:T(1024)S(1)} %copy-done.16, f32[3072]{0:T(1024)S(1)} %broadcast_add_fusion, f32[256]{0:T(256)S(1)} %add_rsqrt_fusion.1, f32[256]{0:T(256)S(1)} %broadcast_multiply_fusion.1), kind=kOutput, calls=%fused_computation.21 | convolution fusion | flops 3628597248 | bytes 18114560 | tf_op jit(solution)/shard_map/td,dcn->ctn/dot_general | solution.py:46
  65.4 1.5 head_norm.3
  68.4 22.4 %all-gather.2.cloned.1.call-done = bf16[16,6,8,3072]{3,2,1,0:T(8,128)(2,1)} async-done(((bf16[16,6,8,768]{3,2,1,0:T(8,128)(2,1)}), bf16[16,6,8,3072]{3,2,1,0:T(8,128)(2,1)}) %all-gather.2.cloned.1.call-update) | async-done | bytes 4718608 | tf_op jit(solution)/shard_map/all_gather | solution.py:150
  90.8 3.2 %convert_reduce_fusion = f32[16,6,8]{2,1,0:T(8,128)S(1)} fusion(bf16[16,6,8,3072]{3,2,1,0:T(8,128)(2,1)} %all-gather.2.cloned.1.call-done), kind=kLoop, calls=%fused_computation.2 | loop fusion | flops 4717824 | bytes 4721664 | tf_op jit(solution)/shard_map/reduce_sum | solution.py:26
  94.5 1.4 fusion.2
  95.9 2.7 fusion.5
  99.5 11.3 %convolution_bitcast_fusion.product_ref = f32[3,768,768]{2,1,0:T(8,128)S(1)} fusion(bf16[768,3072,1]{1,0,2:T(8,128)(2,1)S(1)} %bitcast.56, bf16[3072,3,768]{2,0,1:T(8,128)(2,1)S(1)} %copy-done.20), kind=kOutput, calls=%fused_computation.18 | convolution fusion | flops 10871635968 | bytes 25952256 | tf_op jit(solution)/shard_map/td,dcn->ctn/dot_general | solution.py:46
  110.9 2.8 head_norm.2
  113.8 4.9 %text_attention.1 = (bf16[256,768]{1,0:T(8,128)(2,1)S(1)}, f32[256,768]{1,0:T(8,128)S(1)}) custom-call(bf16[256,768]{1,0:T(8,128)(2,1)S(1)} %copy-done.6, bf16[768,768]{1,0:T(8,128)(2,1)S(1)} %get-tuple-element.11.own_k, bf16[768,768]{1,0:T(8,128)(2,1)S(1)} %get-tuple-element.12.own_v, bf16[256,768]{1,0:T(8,128)(2,1)S(1)} %get-tuple-element.13.text_k, ...), custom_call_target="tpu_custom_call" | custom-call | flops 805306368 | bytes 6291456 | tf_op jit(solution)/shard_map/text_attention/pallas_call | solution.py:180
  121.4 1.5 collective-permute-start.4
  124.2 4.5 %collective-permute-start = (bf16[768,768]{1,0:T(8,128)(2,1)S(1)}, bf16[768,768]{1,0:T(8,128)(2,1)}, u32[]{:S(2)}, u32[]{:S(2)}) collective-permute-start(bf16[768,768]{1,0:T(8,128)(2,1)S(1)} %get-tuple-element.11.own_k), channel_id=1, source_target_pairs={{0,4},{4,8},{8,12},{1,5},{5,9},{9,13},{2,6},{6,10},{10,14},{3,7},{... | collective-permute-start | bytes 3538952 | tf_op jit(solution)/shard_map/ppermute | solution.py:163
  128.6 3.4 %collective-permute-start.1 = (bf16[768,768]{1,0:T(8,128)(2,1)S(1)}, bf16[768,768]{1,0:T(8,128)(2,1)}, u32[]{:S(2)}, u32[]{:S(2)}) collective-permute-start(bf16[768,768]{1,0:T(8,128)(2,1)S(1)} %get-tuple-element.12.own_v), channel_id=1, source_target_pairs={{0,4},{4,8},{8,12},{1,5},{5,9},{9,13},{2,6},{6,10},{10,14},{3,7},{... | collective-permute-start | bytes 3538952 | tf_op jit(solution)/shard_map/ppermute | solution.py:163
  132.0 1.3 collective-permute-start.2
  133.3 1.3 collective-permute-start.3
  135.6 2.3 copy.29
  138.9 2.3 copy.30
  141.2 4.7 %collective-permute-start.6 = (f32[256,6]{0,1:T(8,128)S(1)}, f32[256,6]{0,1:T(8,128)S(1)}, u32[]{:S(2)}, u32[]{:S(2)}) collective-permute-start(f32[256,6]{0,1:T(8,128)S(1)} %get-tuple-element.21), channel_id=1, source_target_pairs={{0,8},{4,12},{8,0},{12,4},{1,9},{5,13},{9,1},{13,5},{2,10},{6,14},... | collective-permute-start | bytes 18440 | tf_op jit(solution)/shard_map/ppermute | solution.py:203
  145.9 2.4 add_convert_fusion.1
  148.3 38.0 %collective-permute-done.6 = f32[256,6]{0,1:T(8,128)S(1)} collective-permute-done((f32[256,6]{0,1:T(8,128)S(1)}, f32[256,6]{0,1:T(8,128)S(1)}, u32[]{:S(2)}, u32[]{:S(2)}) %collective-permute-start.6) | collective-permute-done | bytes 6176 | tf_op jit(solution)/shard_map/ppermute | solution.py:203
  187.5 2.4 copy.31
  190.8 2.3 copy.32
  193.1 11.8 %collective-permute-done.7 = bf16[256,768]{1,0:T(8,128)(2,1)} collective-permute-done((bf16[256,768]{1,0:T(8,128)(2,1)}, bf16[256,768]{1,0:T(8,128)(2,1)}, u32[]{:S(2)}, u32[]{:S(2)}) %collective-permute-start.7) | collective-permute-done | bytes 393248 | tf_op jit(solution)/shard_map/ppermute | solution.py:202
  204.9 1.7 add_convert_fusion
  206.7 1.3 copy-done.10
  207.9 16.6 %latent_attention.1 = bf16[768,768]{1,0:T(8,128)(2,1)S(1)} custom-call(s32[3,4]{1,0:T(4,128)S(1)} %pad_add_fusion.rows_ref, bf16[768,768]{1,0:T(8,128)(2,1)S(1)} %copy-done.10, bf16[768,768]{1,0:T(8,128)(2,1)S(1)} %get-tuple-element.11.own_k, bf16[768,768]{1,0:T(8,128)(2,1)S(1)} %get-tuple-element.12.own_v, bf16[768,768]{1,0:T(8,128)(2,1)} %collective-permute-done.low_k, ...), custom_call_target="tpu_custom_call" | custom-call | flops 4227858432 | bytes 10485760 | tf_op jit(solution)/shard_map/latent_attention/pallas_call | solution.py:222
  224.6 9.3 %convolution_convert_fusion = bf16[1024,3072]{1,0:T(8,128)(2,1)} fusion(bf16[1024,768]{1,0:T(8,128)(2,1)S(1)} %bitcast.62, bf16[768,3072]{1,0:T(8,128)(2,1)} %param.18), kind=kOutput, calls=%fused_computation.9 | convolution fusion | flops 4834983936 | bytes 12582912 | tf_op jit(solution)/shard_map/dot_general | solution.py:246
  234.0 56.9 %reduce-scatter.2.cloned.1.call-done = bf16[256,3072]{1,0:T(8,128)(2,1)} async-done(((bf16[1024,3072]{1,0:T(8,128)(2,1)}), bf16[256,3072]{1,0:T(8,128)(2,1)}) %reduce-scatter.2.cloned.1.call-update) | async-done | bytes 1572880 | tf_op jit(solution)/shard_map/reduce_scatter | solution.py:245
  290.8 1.8 convert_element_type.53
  292.6 1.2 fusion.12
  (83 shorter events, 14.5 us)
Async XLA Ops:
  7.2 83.6 %all-gather.2.cloned.1.call-start = ((), (), s32[]{:S(2)}) async-start(), calls=%async_computation.2 | async-start | bytes 5898240 | tf_op jit(solution)/shard_map/all_gather | solution.py:150
  9.1 44.9 %copy-start.17 = (s32[2,4]{1,0:T(2,128)S(1)}, s32[2,4]{1,0:T(2,128)}, u32[]{:S(2)}) copy-start(s32[2,4]{1,0:T(2,128)} %param.21) | copy-start | bytes 100
  9.2 45.0 %copy-start.11 = (s32[8]{0:T(128)S(1)}, s32[8]{0:T(128)}, u32[]{:S(2)}) copy-start(s32[8]{0:T(128)} %param.22) | copy-start | bytes 100
  52.3 3.3 %copy-start.13 = (bf16[256,3072]{1,0:T(8,128)(2,1)S(1)}, bf16[256,3072]{1,0:T(8,128)(2,1)}, u32[]{:S(2)}) copy-start(bf16[256,3072]{1,0:T(8,128)(2,1)} %param.13) | copy-start | bytes 4718596
  53.9 2.5 copy-start.15
  53.9 2.5 copy-start.16
  53.9 236.9 %reduce-scatter.2.cloned.1.call-start = ((), (), s32[]{:S(2)}) async-start(), calls=%async_computation.3 | async-start | bytes 7864320 | tf_op jit(solution)/shard_map/reduce_scatter | solution.py:245
  56.5 8.9 %copy-start.7 = (f32[128]{0:T(128)S(1)}, f32[128]{0:T(128)}, u32[]{:S(2)}) copy-start(f32[128]{0:T(128)} %param.19) | copy-start | bytes 1540
  56.5 8.9 %copy-start.8 = (f32[128]{0:T(128)S(1)}, f32[128]{0:T(128)}, u32[]{:S(2)}) copy-start(f32[128]{0:T(128)} %param.20) | copy-start | bytes 1540
  56.5 11.9 %copy-start.19 = (s32[256]{0:T(256)S(1)}, s32[256]{0:T(256)}, u32[]{:S(2)}) copy-start(s32[256]{0:T(256)} %param.23) | copy-start | bytes 3076
  66.9 0.7 copy-start
  67.6 0.7 copy-start.5
  90.8 3.8 %copy-start.12 = (bf16[16,6,8,3072]{3,2,1,0:T(8,128)(2,1)S(1)}, bf16[16,6,8,3072]{3,2,1,0:T(8,128)(2,1)}, u32[]{:S(2)}) copy-start(bf16[16,6,8,3072]{3,2,1,0:T(8,128)(2,1)} %all-gather.2.cloned.1.call-done) | copy-start | bytes 14155780
  94.5 5.0 %copy-start.20 = (bf16[3072,3,768]{2,0,1:T(8,128)(2,1)S(1)}, bf16[3072,3,768]{2,0,1:T(8,128)(2,1)}, u32[]{:S(2)}) copy-start(bf16[3072,3,768]{2,0,1:T(8,128)(2,1)} %param.17) | copy-start | bytes 42467332
  110.9 2.9 copy-start.1
  110.9 2.9 copy-start.6
  113.7 4.9 %copy-start.9 = (bf16[768,768]{1,0:T(8,128)(2,1)}, bf16[768,768]{1,0:T(8,128)(2,1)S(1)}, u32[]{:S(2)}) copy-start(bf16[768,768]{1,0:T(8,128)(2,1)S(1)} %get-tuple-element.10.q_ref) | copy-start | bytes 3538948
  118.7 0.7 copy-start.3
  120.6 25.3 %copy-start.4 = (bf16[256,768]{1,0:T(8,128)(2,1)S(1)}, bf16[256,768]{1,0:T(8,128)(2,1)}, u32[]{:S(2)}) copy-start(bf16[256,768]{1,0:T(8,128)(2,1)} %copy-done.3) | copy-start | bytes 1179652
  121.4 11.9 %collective-permute-start.4 = (f32[256,6]{0,1:T(8,128)S(1)}, f32[256,6]{0,1:T(8,128)S(1)}, u32[]{:S(2)}, u32[]{:S(2)}) collective-permute-start(f32[256,6]{0,1:T(8,128)S(1)} %bitcast.66), channel_id=1, source_target_pairs={{0,4},{4,0},{8,12},{12,8},{1,5},{5,1},{9,13},{13,9},{2,6},{6,2},{1... | collective-permute-start | bytes 18440 | tf_op jit(solution)/shard_map/ppermute | solution.py:203
  122.9 18.3 %collective-permute-start.5 = (bf16[256,768]{1,0:T(8,128)(2,1)}, bf16[256,768]{1,0:T(8,128)(2,1)}, u32[]{:S(2)}, u32[]{:S(2)}) collective-permute-start(bf16[256,768]{1,0:T(8,128)(2,1)} %copy-done.3), channel_id=1, source_target_pairs={{0,4},{4,0},{8,12},{12,8},{1,5},{5,1},{9,13},{13,9},{2,6},{6,2},{1... | collective-permute-start | bytes 1179656 | tf_op jit(solution)/shard_map/ppermute | solution.py:202
  124.2 82.4 %collective-permute-start = (bf16[768,768]{1,0:T(8,128)(2,1)S(1)}, bf16[768,768]{1,0:T(8,128)(2,1)}, u32[]{:S(2)}, u32[]{:S(2)}) collective-permute-start(bf16[768,768]{1,0:T(8,128)(2,1)S(1)} %get-tuple-element.11.own_k), channel_id=1, source_target_pairs={{0,4},{4,8},{8,12},{1,5},{5,9},{9,13},{2,6},{6,10},{10,14},{3,7},{... | collective-permute-start | bytes 3538952 | tf_op jit(solution)/shard_map/ppermute | solution.py:163
  128.6 78.0 %collective-permute-start.1 = (bf16[768,768]{1,0:T(8,128)(2,1)S(1)}, bf16[768,768]{1,0:T(8,128)(2,1)}, u32[]{:S(2)}, u32[]{:S(2)}) collective-permute-start(bf16[768,768]{1,0:T(8,128)(2,1)S(1)} %get-tuple-element.12.own_v), channel_id=1, source_target_pairs={{0,4},{4,8},{8,12},{1,5},{5,9},{9,13},{2,6},{6,10},{10,14},{3,7},{... | collective-permute-start | bytes 3538952 | tf_op jit(solution)/shard_map/ppermute | solution.py:163
  132.0 74.6 %collective-permute-start.2 = (bf16[768,768]{1,0:T(8,128)(2,1)S(1)}, bf16[768,768]{1,0:T(8,128)(2,1)}, u32[]{:S(2)}, u32[]{:S(2)}) collective-permute-start(bf16[768,768]{1,0:T(8,128)(2,1)S(1)} %get-tuple-element.11.own_k), channel_id=1, source_target_pairs={{4,0},{8,4},{12,8},{5,1},{9,5},{13,9},{6,2},{10,6},{14,10},{7,3},{... | collective-permute-start | bytes 3538952 | tf_op jit(solution)/shard_map/ppermute | solution.py:164
  133.3 73.3 %collective-permute-start.3 = (bf16[768,768]{1,0:T(8,128)(2,1)S(1)}, bf16[768,768]{1,0:T(8,128)(2,1)}, u32[]{:S(2)}, u32[]{:S(2)}) collective-permute-start(bf16[768,768]{1,0:T(8,128)(2,1)S(1)} %get-tuple-element.12.own_v), channel_id=1, source_target_pairs={{4,0},{8,4},{12,8},{5,1},{9,5},{13,9},{6,2},{10,6},{14,10},{7,3},{... | collective-permute-start | bytes 3538952 | tf_op jit(solution)/shard_map/ppermute | solution.py:164
  135.6 50.9 %copy-start.18 = (s32[2,4]{1,0:T(2,128)S(1)}, s32[2,4]{1,0:T(2,128)}, u32[]{:S(2)}) copy-start(s32[2,4]{1,0:T(2,128)} %param.21) | copy-start | bytes 100
  141.2 45.2 %collective-permute-start.6 = (f32[256,6]{0,1:T(8,128)S(1)}, f32[256,6]{0,1:T(8,128)S(1)}, u32[]{:S(2)}, u32[]{:S(2)}) collective-permute-start(f32[256,6]{0,1:T(8,128)S(1)} %get-tuple-element.21), channel_id=1, source_target_pairs={{0,8},{4,12},{8,0},{12,4},{1,9},{5,13},{9,1},{13,5},{2,10},{6,14},... | collective-permute-start | bytes 18440 | tf_op jit(solution)/shard_map/ppermute | solution.py:203
  186.4 18.5 %collective-permute-start.7 = (bf16[256,768]{1,0:T(8,128)(2,1)}, bf16[256,768]{1,0:T(8,128)(2,1)}, u32[]{:S(2)}, u32[]{:S(2)}) collective-permute-start(bf16[256,768]{1,0:T(8,128)(2,1)} %add_convert_fusion.1), channel_id=1, source_target_pairs={{0,8},{4,12},{8,0},{12,4},{1,9},{5,13},{9,1},{13,5},{2,10},{6,14},... | collective-permute-start | bytes 1179656 | tf_op jit(solution)/shard_map/ppermute | solution.py:202
  187.5 19.2 %copy-start.2 = (bf16[256,768]{1,0:T(8,128)(2,1)S(1)}, bf16[256,768]{1,0:T(8,128)(2,1)}, u32[]{:S(2)}) copy-start(bf16[256,768]{1,0:T(8,128)(2,1)} %copy-done) | copy-start | bytes 1179652
  206.6 1.3 copy-start.10
  234.0 58.7 %copy-start.14 = (f32[3072]{0:T(1024)S(1)}, f32[3072]{0:T(1024)}, u32[]{:S(2)}) copy-start(f32[3072]{0:T(1024)} %param.16) | copy-start | bytes 36868
Sparse Core Ops, SparseCore 0:
  54.1 36.6 all-gather.1
  234.1 56.7 reduce-scatter.1

commit v2 on v1

--- a/solution.py
+++ b/solution.py
@@ -241,13 +241,33 @@
     latent_columns = latent_out.reshape(head_count, -1, width)
     text_blocks = text_part.reshape(head_count, -1, width)
     latent_share = latent_columns.shape[1]
-    joined = jnp.concatenate([latent_columns, text_blocks], 1).reshape(-1, width)
-    summed_rows = lax.psum_scatter(
-        jnp.dot(joined, project_out, preferred_element_type=jnp.float32).astype(jnp.bfloat16),
-        "head",
-        scatter_dimension=0,
-        tiled=True,
-    ).astype(jnp.float32)
+    blocks = jnp.concatenate([latent_columns, text_blocks], 1)
+    share = blocks.shape[1]
+    bits = head_count.bit_length() - 1
+    order = tuple(reversed(range(bits))) + (bits, bits + 1)
+    joined = jnp.transpose(blocks.reshape((2,) * bits + (share, width)), order)
+    joined = joined.reshape(2, -1, width)
+    head_index = lax.axis_index("head")
+    kept_total = None
+    for step in range(bits):
+        mine = (head_index >> step) & 1
+        pairs = [(i, i ^ (1 << step)) for i in range(head_count)]
+        if step == 0:
+
+            def project(half):
+                rows = lax.dynamic_index_in_dim(joined, half, 0, keepdims=False)
+                term = jnp.dot(rows, project_out, preferred_element_type=jnp.float32)
+                return term.astype(jnp.bfloat16)
+
+            sent, kept = project(1 - mine), project(mine)
+        else:
+            halves = kept_total.reshape(2, -1, D)
+            sent = lax.dynamic_index_in_dim(halves, 1 - mine, 0, keepdims=False)
+            kept = lax.dynamic_index_in_dim(halves, mine, 0, keepdims=False)
+            sent = sent.astype(jnp.bfloat16)
+        arrived = lax.ppermute(sent, "head", pairs)
+        kept_total = kept.astype(jnp.float32) + arrived.astype(jnp.float32)
+    summed_rows = kept_total
     update = (
         (summed_rows[:latent_share] * mod_gate)
         .astype(jnp.bfloat16)

time: 302 us -> 294 us (0.974)
  waiting for transfers between devices: 129 us -> 114 us
    reduce_scatter x1 -> x0, waiting for transfers between devices: 56.9 us -> none  [shards(): lax.psum_scatter(jnp.dot(joined, project_out, preferred_element_type=jnp....]
    ppermute x0 -> x2, waiting for transfers between devices: none -> 41.9 us  [shards(): arrived = lax.ppermute(sent, 'head', pairs)]
    dot_general x1 -> x2, matrix products: 9.31 us -> 12.2 us  [project(): term = jnp.dot(rows, project_out, preferred_element_type=jnp.float32)]
    unnamed x45 -> x47, local copies, waits for them, and re-layouts: 7.02 us -> 9.64 us
  transfers between devices with their start and end apart: 10 -> 11, of which waited for: 4 -> 5; matrix products, arithmetic and copies ran while one was open for 10% -> 10% of each run, Pallas kernels for 1% -> 1%
where the time goes in v2:
time: 294 us
  waiting for transfers between devices  114 us (39%)
  blocking collectives  43.1 us (15%)
  matrix products  32.4 us (11%)
  local copies, waits for them, and re-layouts  28.2 us (10%)
  Pallas kernels  25.8 us (9%)
  starting transfers between devices  17.8 us (6%)
  other arithmetic  17.6 us (6%)
  between operations  14.4 us (5%)
    all_to_all x1, blocking collectives, shards(): lax.all_to_all(latent, 'tile', split_axis=2, concat_axis=0, tiled=True)  43.1 us
    ppermute x2, waiting for transfers between devices, shards(): arrived = lax.ppermute(sent, 'head', pairs)  41.9 us
    ppermute x2, waiting for transfers between devices, shards(): other_level = lax.ppermute(level, 'tile', pairs)  38.1 us
    all_gather x1, waiting for transfers between devices, shards(): column_whole = lax.all_gather(moved, 'head', axis=3, tiled=True)  22.4 us
    dot_general x2, matrix products, prepare(): jnp.einsum('td,dcn->ctn', normed, project_in, preferred_element_type=jnp....  20.2 us
    pallas_call x1, Pallas kernels, shards(): pl.pallas_call(functools.partial(latent_kernel, per_device, tile_size, sl...  16.6 us
    dot_general x2, matrix products, project(): term = jnp.dot(rows, project_out, preferred_element_type=jnp.float32)  12.2 us
    ppermute x2, waiting for transfers between devices, shards(): other_part = lax.ppermute(text_part, 'tile', pairs)  11.8 us
  transfers between devices with their start and end apart: 11, of which 5 were waited for; matrix products, arithmetic and copies ran while one was open for 10% of the time, Pallas kernels for 1%

profile of v2, /device:TPU:0, one launch (start us, length us, event | category | flops | bytes accessed | tf_op | source)
XLA Modules:
  0.0 293.5 jit_solution(8845407360061365085)
XLA Ops:
  7.2 1.9 copy.29
  9.2 43.1 %all_to_all.18 = bf16[4,6,32,768]{3,1,0,2:T(8,128)(2,1)S(1)} all-to-all(bf16[4,6,32,768]{3,1,0,2:T(8,128)(2,1)S(1)} %copy.29), channel_id=1, replica_groups=mesh['group'=2,'tile'=4,'head'=4] {'tile'}, dimensions={2} | all-to-all | bytes 2359296 | tf_op jit(solution)/shard_map/all_to_all | solution.py:149
  52.3 1.7 copy.31
  56.5 8.9 %convolution_bitcast_fusion.1.product_ref = f32[3,256,768]{2,1,0:T(8,128)S(1)} fusion(bf16[3072,3,768]{2,0,1:T(8,128)(2,1)} %param.17, bf16[256,3072]{1,0:T(8,128)(2,1)} %param.13, f32[3072]{0:T(1024)S(1)} %copy-done.17, f32[3072]{0:T(1024)S(1)} %broadcast_add_fusion, f32[256]{0:T(256)S(1)} %add_rsqrt_fusion.1, f32[256]{0:T(256)S(1)} %broadcast_multiply_fusion.1), kind=kOutput, calls=%fused_computation.25 | convolution fusion | flops 3628597248 | bytes 18114560 | tf_op jit(solution)/shard_map/td,dcn->ctn/dot_general | solution.py:46
  65.4 1.5 head_norm.3
  68.4 22.4 %all-gather.2.cloned.1.call-done = bf16[16,6,8,3072]{3,2,1,0:T(8,128)(2,1)} async-done(((bf16[16,6,8,768]{3,2,1,0:T(8,128)(2,1)}), bf16[16,6,8,3072]{3,2,1,0:T(8,128)(2,1)}) %all-gather.2.cloned.1.call-update) | async-done | bytes 4718608 | tf_op jit(solution)/shard_map/all_gather | solution.py:150
  90.7 3.2 %convert_reduce_fusion = f32[16,6,8]{2,1,0:T(8,128)S(1)} fusion(bf16[16,6,8,3072]{3,2,1,0:T(8,128)(2,1)} %all-gather.2.cloned.1.call-done), kind=kLoop, calls=%fused_computation.2 | loop fusion | flops 4717824 | bytes 4721664 | tf_op jit(solution)/shard_map/reduce_sum | solution.py:26
  94.5 1.4 fusion.2
  95.9 2.7 fusion.5
  99.5 11.3 %convolution_bitcast_fusion.product_ref = f32[3,768,768]{2,1,0:T(8,128)S(1)} fusion(bf16[768,3072,1]{1,0,2:T(8,128)(2,1)S(1)} %bitcast.69, bf16[3072,3,768]{2,0,1:T(8,128)(2,1)S(1)} %copy-done.21), kind=kOutput, calls=%fused_computation.22 | convolution fusion | flops 10871635968 | bytes 25952256 | tf_op jit(solution)/shard_map/td,dcn->ctn/dot_general | solution.py:46
  110.8 2.8 head_norm.2
  113.7 4.9 %text_attention.1 = (bf16[256,768]{1,0:T(8,128)(2,1)S(1)}, f32[256,768]{1,0:T(8,128)S(1)}) custom-call(bf16[256,768]{1,0:T(8,128)(2,1)S(1)} %copy-done.6, bf16[768,768]{1,0:T(8,128)(2,1)S(1)} %get-tuple-element.11.own_k, bf16[768,768]{1,0:T(8,128)(2,1)S(1)} %get-tuple-element.12.own_v, bf16[256,768]{1,0:T(8,128)(2,1)S(1)} %get-tuple-element.13.text_k, ...), custom_call_target="tpu_custom_call" | custom-call | flops 805306368 | bytes 6291456 | tf_op jit(solution)/shard_map/text_attention/pallas_call | solution.py:180
  121.4 1.5 collective-permute-start.4
  124.2 4.4 %collective-permute-start = (bf16[768,768]{1,0:T(8,128)(2,1)S(1)}, bf16[768,768]{1,0:T(8,128)(2,1)}, u32[]{:S(2)}, u32[]{:S(2)}) collective-permute-start(bf16[768,768]{1,0:T(8,128)(2,1)S(1)} %get-tuple-element.11.own_k), channel_id=1, source_target_pairs={{0,4},{4,8},{8,12},{1,5},{5,9},{9,13},{2,6},{6,10},{10,14},{3,7},{... | collective-permute-start | bytes 3538952 | tf_op jit(solution)/shard_map/ppermute | solution.py:163
  128.6 3.4 %collective-permute-start.1 = (bf16[768,768]{1,0:T(8,128)(2,1)S(1)}, bf16[768,768]{1,0:T(8,128)(2,1)}, u32[]{:S(2)}, u32[]{:S(2)}) collective-permute-start(bf16[768,768]{1,0:T(8,128)(2,1)S(1)} %get-tuple-element.12.own_v), channel_id=1, source_target_pairs={{0,4},{4,8},{8,12},{1,5},{5,9},{9,13},{2,6},{6,10},{10,14},{3,7},{... | collective-permute-start | bytes 3538952 | tf_op jit(solution)/shard_map/ppermute | solution.py:163
  133.3 1.3 collective-permute-start.3
  135.6 2.3 copy.33
  138.8 2.3 copy.34
  141.1 4.7 %collective-permute-start.6 = (f32[256,6]{0,1:T(8,128)S(1)}, f32[256,6]{0,1:T(8,128)S(1)}, u32[]{:S(2)}, u32[]{:S(2)}) collective-permute-start(f32[256,6]{0,1:T(8,128)S(1)} %get-tuple-element.21), channel_id=1, source_target_pairs={{0,8},{4,12},{8,0},{12,4},{1,9},{5,13},{9,1},{13,5},{2,10},{6,14},... | collective-permute-start | bytes 18440 | tf_op jit(solution)/shard_map/ppermute | solution.py:203
  145.9 2.4 add_convert_fusion.1
  148.3 38.1 %collective-permute-done.6 = f32[256,6]{0,1:T(8,128)S(1)} collective-permute-done((f32[256,6]{0,1:T(8,128)S(1)}, f32[256,6]{0,1:T(8,128)S(1)}, u32[]{:S(2)}, u32[]{:S(2)}) %collective-permute-start.6) | collective-permute-done | bytes 6176 | tf_op jit(solution)/shard_map/ppermute | solution.py:203
  187.4 2.4 copy.35
  190.7 2.3 copy.36
  193.0 11.8 %collective-permute-done.7 = bf16[256,768]{1,0:T(8,128)(2,1)} collective-permute-done((bf16[256,768]{1,0:T(8,128)(2,1)}, bf16[256,768]{1,0:T(8,128)(2,1)}, u32[]{:S(2)}, u32[]{:S(2)}) %collective-permute-start.7) | collective-permute-done | bytes 393248 | tf_op jit(solution)/shard_map/ppermute | solution.py:202
  204.8 1.7 add_convert_fusion
  207.9 16.6 %latent_attention.1 = bf16[768,768]{1,0:T(8,128)(2,1)S(1)} custom-call(s32[3,4]{1,0:T(4,128)S(1)} %pad_add_fusion.rows_ref, bf16[768,768]{1,0:T(8,128)(2,1)S(1)} %copy-done.10, bf16[768,768]{1,0:T(8,128)(2,1)S(1)} %get-tuple-element.11.own_k, bf16[768,768]{1,0:T(8,128)(2,1)S(1)} %get-tuple-element.12.own_v, bf16[768,768]{1,0:T(8,128)(2,1)} %collective-permute-done.low_k, ...), custom_call_target="tpu_custom_call" | custom-call | flops 4227858432 | bytes 10485760 | tf_op jit(solution)/shard_map/latent_attention/pallas_call | solution.py:222
  224.7 6.3 %convolution_convert_fusion = bf16[512,3072]{1,0:T(8,128)(2,1)} fusion(bf16[768,3072]{1,0:T(8,128)(2,1)} %param.18, bf16[2,512,768]{2,1,0:T(8,128)(2,1)S(1)} %bitcast.77, s32[]{:T(128)S(6)} %select_n.83), kind=kOutput, calls=%fused_computation.10 | convolution fusion | flops 2417491968 | bytes 8650756 | tf_op jit(solution)/shard_map/dot_general | solution.py:259
  231.0 6.0 %collective-permute-done.8 = bf16[512,3072]{1,0:T(8,128)(2,1)} collective-permute-done((bf16[512,3072]{1,0:T(8,128)(2,1)}, bf16[512,3072]{1,0:T(8,128)(2,1)}, u32[]{:S(2)}, u32[]{:S(2)}) %collective-permute-start.8) | collective-permute-done | bytes 3145760 | tf_op jit(solution)/shard_map/ppermute | solution.py:268
  237.0 5.9 %convert_add_fusion = f32[512,3072]{1,0:T(8,128)S(1)} fusion(bf16[512,3072]{1,0:T(8,128)(2,1)} %collective-permute-done.8, bf16[768,3072]{1,0:T(8,128)(2,1)} %param.18, bf16[2,512,768]{2,1,0:T(8,128)(2,1)S(1)} %bitcast.78, s32[]{:T(128)S(6)} %select_n.82), kind=kOutput, calls=%fused_computation.9 | convolution fusion | flops 2422210560 | bytes 14942212 | tf_op jit(solution)/shard_map/dot_general | solution.py:259
  243.0 2.6 copy-done.14
  246.4 35.9 %collective-permute-done.9 = bf16[256,3072]{1,0:T(8,128)(2,1)S(1)} collective-permute-done((bf16[256,3072]{1,0:T(8,128)(2,1)S(1)}, bf16[256,3072]{1,0:T(8,128)(2,1)S(1)}, u32[]{:S(2)}, u32[]{:S(2)}) %collective-permute-start.9) | collective-permute-done | bytes 1572896 | tf_op jit(solution)/shard_map/ppermute | solution.py:268
  282.3 2.4 bitcast_add_fusion
  (89 shorter events, 19.1 us)
Async XLA Ops:
  7.2 83.6 %all-gather.2.cloned.1.call-start = ((), (), s32[]{:S(2)}) async-start(), calls=%async_computation.1 | async-start | bytes 5898240 | tf_op jit(solution)/shard_map/all_gather | solution.py:150
  9.1 44.8 %copy-start.18 = (s32[2,4]{1,0:T(2,128)S(1)}, s32[2,4]{1,0:T(2,128)}, u32[]{:S(2)}) copy-start(s32[2,4]{1,0:T(2,128)} %param.21) | copy-start | bytes 100
  9.2 44.9 %copy-start.11 = (s32[8]{0:T(128)S(1)}, s32[8]{0:T(128)}, u32[]{:S(2)}) copy-start(s32[8]{0:T(128)} %param.22) | copy-start | bytes 100
  52.3 3.3 %copy-start.13 = (bf16[256,3072]{1,0:T(8,128)(2,1)S(1)}, bf16[256,3072]{1,0:T(8,128)(2,1)}, u32[]{:S(2)}) copy-start(bf16[256,3072]{1,0:T(8,128)(2,1)} %param.13) | copy-start | bytes 4718596
  53.9 2.5 copy-start.16
  53.9 2.5 copy-start.17
  56.4 8.9 %copy-start.7 = (f32[128]{0:T(128)S(1)}, f32[128]{0:T(128)}, u32[]{:S(2)}) copy-start(f32[128]{0:T(128)} %param.19) | copy-start | bytes 1540
  56.4 8.9 %copy-start.8 = (f32[128]{0:T(128)S(1)}, f32[128]{0:T(128)}, u32[]{:S(2)}) copy-start(f32[128]{0:T(128)} %param.20) | copy-start | bytes 1540
  56.5 11.9 %copy-start.20 = (s32[256]{0:T(256)S(1)}, s32[256]{0:T(256)}, u32[]{:S(2)}) copy-start(s32[256]{0:T(256)} %param.23) | copy-start | bytes 3076
  67.6 0.7 copy-start.5
  90.7 3.8 %copy-start.12 = (bf16[16,6,8,3072]{3,2,1,0:T(8,128)(2,1)S(1)}, bf16[16,6,8,3072]{3,2,1,0:T(8,128)(2,1)}, u32[]{:S(2)}) copy-start(bf16[16,6,8,3072]{3,2,1,0:T(8,128)(2,1)} %all-gather.2.cloned.1.call-done) | copy-start | bytes 14155780
  94.5 5.0 %copy-start.21 = (bf16[3072,3,768]{2,0,1:T(8,128)(2,1)S(1)}, bf16[3072,3,768]{2,0,1:T(8,128)(2,1)}, u32[]{:S(2)}) copy-start(bf16[3072,3,768]{2,0,1:T(8,128)(2,1)} %param.17) | copy-start | bytes 42467332
  110.8 2.9 copy-start.1
  110.8 2.9 copy-start.6
  113.7 4.9 %copy-start.9 = (bf16[768,768]{1,0:T(8,128)(2,1)}, bf16[768,768]{1,0:T(8,128)(2,1)S(1)}, u32[]{:S(2)}) copy-start(bf16[768,768]{1,0:T(8,128)(2,1)S(1)} %get-tuple-element.10.q_ref) | copy-start | bytes 3538948
  118.6 0.7 copy-start.3
  120.5 25.3 %copy-start.4 = (bf16[256,768]{1,0:T(8,128)(2,1)S(1)}, bf16[256,768]{1,0:T(8,128)(2,1)}, u32[]{:S(2)}) copy-start(bf16[256,768]{1,0:T(8,128)(2,1)} %copy-done.3) | copy-start | bytes 1179652
  121.4 11.9 %collective-permute-start.4 = (f32[256,6]{0,1:T(8,128)S(1)}, f32[256,6]{0,1:T(8,128)S(1)}, u32[]{:S(2)}, u32[]{:S(2)}) collective-permute-start(f32[256,6]{0,1:T(8,128)S(1)} %bitcast.82), channel_id=1, source_target_pairs={{0,4},{4,0},{8,12},{12,8},{1,5},{5,1},{9,13},{13,9},{2,6},{6,2},{1... | collective-permute-start | bytes 18440 | tf_op jit(solution)/shard_map/ppermute | solution.py:203
  122.9 18.3 %collective-permute-start.5 = (bf16[256,768]{1,0:T(8,128)(2,1)}, bf16[256,768]{1,0:T(8,128)(2,1)}, u32[]{:S(2)}, u32[]{:S(2)}) collective-permute-start(bf16[256,768]{1,0:T(8,128)(2,1)} %copy-done.3), channel_id=1, source_target_pairs={{0,4},{4,0},{8,12},{12,8},{1,5},{5,1},{9,13},{13,9},{2,6},{6,2},{1... | collective-permute-start | bytes 1179656 | tf_op jit(solution)/shard_map/ppermute | solution.py:202
  124.2 82.4 %collective-permute-start = (bf16[768,768]{1,0:T(8,128)(2,1)S(1)}, bf16[768,768]{1,0:T(8,128)(2,1)}, u32[]{:S(2)}, u32[]{:S(2)}) collective-permute-start(bf16[768,768]{1,0:T(8,128)(2,1)S(1)} %get-tuple-element.11.own_k), channel_id=1, source_target_pairs={{0,4},{4,8},{8,12},{1,5},{5,9},{9,13},{2,6},{6,10},{10,14},{3,7},{... | collective-permute-start | bytes 3538952 | tf_op jit(solution)/shard_map/ppermute | solution.py:163
  128.6 78.0 %collective-permute-start.1 = (bf16[768,768]{1,0:T(8,128)(2,1)S(1)}, bf16[768,768]{1,0:T(8,128)(2,1)}, u32[]{:S(2)}, u32[]{:S(2)}) collective-permute-start(bf16[768,768]{1,0:T(8,128)(2,1)S(1)} %get-tuple-element.12.own_v), channel_id=1, source_target_pairs={{0,4},{4,8},{8,12},{1,5},{5,9},{9,13},{2,6},{6,10},{10,14},{3,7},{... | collective-permute-start | bytes 3538952 | tf_op jit(solution)/shard_map/ppermute | solution.py:163
  132.0 74.6 %collective-permute-start.2 = (bf16[768,768]{1,0:T(8,128)(2,1)S(1)}, bf16[768,768]{1,0:T(8,128)(2,1)}, u32[]{:S(2)}, u32[]{:S(2)}) collective-permute-start(bf16[768,768]{1,0:T(8,128)(2,1)S(1)} %get-tuple-element.11.own_k), channel_id=1, source_target_pairs={{4,0},{8,4},{12,8},{5,1},{9,5},{13,9},{6,2},{10,6},{14,10},{7,3},{... | collective-permute-start | bytes 3538952 | tf_op jit(solution)/shard_map/ppermute | solution.py:164
  133.3 73.3 %collective-permute-start.3 = (bf16[768,768]{1,0:T(8,128)(2,1)S(1)}, bf16[768,768]{1,0:T(8,128)(2,1)}, u32[]{:S(2)}, u32[]{:S(2)}) collective-permute-start(bf16[768,768]{1,0:T(8,128)(2,1)S(1)} %get-tuple-element.12.own_v), channel_id=1, source_target_pairs={{4,0},{8,4},{12,8},{5,1},{9,5},{13,9},{6,2},{10,6},{14,10},{7,3},{... | collective-permute-start | bytes 3538952 | tf_op jit(solution)/shard_map/ppermute | solution.py:164
  135.6 50.9 %copy-start.19 = (s32[2,4]{1,0:T(2,128)S(1)}, s32[2,4]{1,0:T(2,128)}, u32[]{:S(2)}) copy-start(s32[2,4]{1,0:T(2,128)} %param.21) | copy-start | bytes 100
  141.1 45.2 %collective-permute-start.6 = (f32[256,6]{0,1:T(8,128)S(1)}, f32[256,6]{0,1:T(8,128)S(1)}, u32[]{:S(2)}, u32[]{:S(2)}) collective-permute-start(f32[256,6]{0,1:T(8,128)S(1)} %get-tuple-element.21), channel_id=1, source_target_pairs={{0,8},{4,12},{8,0},{12,4},{1,9},{5,13},{9,1},{13,5},{2,10},{6,14},... | collective-permute-start | bytes 18440 | tf_op jit(solution)/shard_map/ppermute | solution.py:203
  186.3 18.5 %collective-permute-start.7 = (bf16[256,768]{1,0:T(8,128)(2,1)}, bf16[256,768]{1,0:T(8,128)(2,1)}, u32[]{:S(2)}, u32[]{:S(2)}) collective-permute-start(bf16[256,768]{1,0:T(8,128)(2,1)} %add_convert_fusion.1), channel_id=1, source_target_pairs={{0,8},{4,12},{8,0},{12,4},{1,9},{5,13},{9,1},{13,5},{2,10},{6,14},... | collective-permute-start | bytes 1179656 | tf_op jit(solution)/shard_map/ppermute | solution.py:202
  187.4 19.2 %copy-start.2 = (bf16[256,768]{1,0:T(8,128)(2,1)S(1)}, bf16[256,768]{1,0:T(8,128)(2,1)}, u32[]{:S(2)}) copy-start(bf16[256,768]{1,0:T(8,128)(2,1)} %copy-done) | copy-start | bytes 1179652
  206.6 1.3 copy-start.10
  231.0 6.0 %collective-permute-start.8 = (bf16[512,3072]{1,0:T(8,128)(2,1)}, bf16[512,3072]{1,0:T(8,128)(2,1)}, u32[]{:S(2)}, u32[]{:S(2)}) collective-permute-start(bf16[512,3072]{1,0:T(8,128)(2,1)} %convolution_convert_fusion), channel_id=1, source_target_pairs={{0,1},{1,0},{2,3},{3,2},{4,5},{5,4},{6,7},{7,6},{8,9},{9,8},{10,11... | collective-permute-start | bytes 9437192 | tf_op jit(solution)/shard_map/ppermute | solution.py:268
  242.9 2.6 copy-start.14
  245.8 36.5 %collective-permute-start.9 = (bf16[256,3072]{1,0:T(8,128)(2,1)S(1)}, bf16[256,3072]{1,0:T(8,128)(2,1)S(1)}, u32[]{:S(2)}, u32[]{:S(2)}) collective-permute-start(bf16[256,3072]{1,0:T(8,128)(2,1)S(1)} %fusion.13), channel_id=1, source_target_pairs={{0,2},{1,3},{2,0},{3,1},{4,6},{5,7},{6,4},{7,5},{8,10},{9,11},{10,... | collective-permute-start | bytes 4718600 | tf_op jit(solution)/shard_map/ppermute | solution.py:268
  246.4 38.3 %copy-start.15 = (f32[3072]{0:T(1024)S(1)}, f32[3072]{0:T(1024)}, u32[]{:S(2)}) copy-start(f32[3072]{0:T(1024)} %param.16) | copy-start | bytes 36868
  (1 other events, 0.7 us)
Sparse Core Ops, SparseCore 0:
  54.1 36.5 all-gather.1
